TPU v7x, 128 devices: a whole 4x4x4 slice. The times are simulated.
128 devices in a mesh: wide: 16 (over z, x), narrow: 8 (over y, core).
Axes of the slice: x: 4, y: 4, z: 4, core: 2. Of those that a mesh axis runs over, the one named last changes fastest.
Arguments:
- solid_density_share: float32 [128, 256, 256], P('wide', 'narrow'), may hold values from 0.1 to 1
- primal_warmth_vector: float32 [128, 256, 256], P('wide', 'narrow'), may hold values from 0.5 to 2
- voxel_aim_scale: float32 [128, 256, 256], P('wide', 'narrow'), may hold values from 0.000375 to 0.009, as said below
- coolant_transfer_factor: float32 [128, 256, 256], P('wide', 'narrow'), may hold values from 0.0003 to 0.003
Outputs:
- adjoint_warmth_vector: float32 [128, 256, 256], P('wide', 'narrow')
- sensitivity: float32 [128, 256, 256], P('wide', 'narrow')
Inputs may be any that keep to these rules, and one draw needn't show every extreme that they name: voxel_aim_scale is positive.
All inputs are finite; a program needn't handle non-finite values.
Results may differ from a plain program's by a relative error of at most 0.0003.
Values sent between devices are 32-bit elements; how exact they have to be, the bound alone decides.
A program may use at most 128 MiB of HBM per device.

v0:
```python
import functools
import math

import jax
import jax.numpy as jnp
from jax import lax
from jax.experimental import pallas as pl
from jax.experimental.pallas import tpu as pltpu
from jax.sharding import PartitionSpec as P

COARSE_ITERS = 8
RADIUS = 4
FLOOR_CONDUCTION = 0.001
OMEGA = 0.7
FILTER_OMEGA = 0.8
STRENGTH = (RADIUS / (2.0 * math.sqrt(3.0))) ** 2
MESH = pl.DeviceIdType.MESH
NW, NN = 16, 8
CELLS = 128 * 256 * 256
F32 = jnp.float32
BF16 = jnp.bfloat16
N_GROUPS = 18
BLANK_TILES = 200
UNROLL = {48: 4, 32: 8}


def near_peers(reach):
    peers = [
        (dw, dn)
        for dw in range(-reach, reach + 1)
        for dn in (-1, 0, 1)
        if (dw, dn) != (0, 0)
    ]
    return sorted(peers, key=lambda p: (p[1] != 0 and p[0] != 0, p[0] == 0, abs(p[0])))


def greeted():
    peers = [(dw % NW, dn % NN) for dw, dn in near_peers(3)]
    peers += [(0, k) for k in range(1, NN)] + [(k, 0) for k in range(1, NW)]
    return sorted(set(peers), key=lambda p: -min(p[0], NW - p[0]) - min(p[1], NN - p[1]))


def layers(lo, hi, body, unroll):
    steps = (hi - lo) // unroll

    def step(k, carry):
        for j in range(unroll):
            body(lo + k * unroll + j)
        return carry

    if steps > 1:
        lax.fori_loop(0, steps, step, 0)
    else:
        step(0, 0) if steps else None
    for i in range(lo + steps * unroll, hi):
        body(i)


class Group:
    def __init__(self, blank, send_sem, recv_sem):
        self.blank, self.send_sem, self.recv_sem = blank, send_sem, recv_sem
        self.tiles = 0

    def wait(self, sem):
        whole = self.blank.at[pl.ds(0, self.tiles)]
        pltpu.make_async_copy(whole, whole, sem).wait()

    def wait_recv(self):
        self.wait(self.recv_sem)


class Wire:
    def __init__(self, wide, narrow, blank, send_sem, recv_sem):
        self.wide, self.narrow, self.blank = wide, narrow, blank
        self.send_sem, self.recv_sem = send_sem, recv_sem
        self.groups = []
        self.sent = 0

    def peer(self, dw, dn):
        return (lax.rem(self.wide + (dw + NW), NW), lax.rem(self.narrow + (dn + NN), NN))

    def group(self):
        k = len(self.groups)
        self.groups.append(Group(self.blank, self.send_sem.at[k], self.recv_sem.at[k]))
        return self.groups[-1]

    def send(self, group, src, dst, dw, dn):
        pltpu.make_async_remote_copy(
            src_ref=src,
            dst_ref=dst,
            send_sem=group.send_sem,
            recv_sem=group.recv_sem,
            device_id=self.peer(dw, dn),
            device_id_type=MESH,
        ).start()
        group.tiles += math.prod(src.shape) // 1024

    def flush(self, last):
        for group in self.groups[self.sent : last]:
            group.wait(group.send_sem)
        self.sent = last


def cut(own, halo, width, shift):
    if shift == 0:
        return pl.ds(halo, own), pl.ds(halo, own)
    if shift > 0:
        return pl.ds(halo + own - width, width), pl.ds(halo - width, width)
    return pl.ds(halo, width), pl.ds(halo + own, width)


def up_y(v):
    return pltpu.roll(v, v.shape[0] - 1, 0)


def down_y(v):
    return pltpu.roll(v, 1, 0)


def up_z(v):
    return pltpu.roll(v, v.shape[1] - 1, 1)


def down_z(v):
    return pltpu.roll(v, 1, 1)


def coupling(u, ux, uy, uz, i):
    centre = u[i]
    fy, fz = uy[i], uz[i]
    return centre, (
        (ux[i] * u[i + 1] + ux[i - 1] * u[i - 1])
        + (fy * up_y(centre) + down_y(fy * centre))
        + (fz * up_z(centre) + down_z(fz * centre))
    )


def sweep(src, dst, rhs, ux, uy, uz, weight, lo, hi):
    def body(i):
        centre, pull = coupling(src, ux, uy, uz, i)
        dst[i] = (1.0 - OMEGA) * centre + weight[i] * (rhs[i] + pull)

    layers(lo, hi, body, UNROLL[src.shape[1]])


def residual_at(src, rhs, ux, uy, uz, diag, i):
    centre, pull = coupling(src, ux, uy, uz, i)
    return rhs[i] + pull - diag[i] * centre


def weights(sink, ux, uy, uz, diag, weight, lo, hi):
    def body(i):
        fy, fz = uy[i], uz[i]
        total = sink[i] + (ux[i] + ux[i - 1]) + (fy + down_y(fy)) + (fz + down_z(fz))
        diag[i] = total
        weight[i] = OMEGA / total

    layers(lo, hi, body, UNROLL[diag.shape[1]])


def next_x(here, above, low):
    return pltpu.roll(jnp.where(low, above, here), 64, 1)


def previous_x(here, below, low):
    return pltpu.roll(jnp.where(low, here, below), 64, 1)


def coupling2(u, ux, uy, uz, t, low):
    centre, above, below = u[t], u[min(t + 1, 6)], max(t - 1, 0)
    fy, fz = uy[t], uz[t]
    return centre, (
        (
            ux[t] * next_x(centre, above, low)
            + previous_x(ux[t] * centre, ux[below] * u[below], low)
        )
        + (fy * up_y(centre) + down_y(fy * centre))
        + (fz * up_z(centre) + down_z(fz * centre))
    )


def sweep2(src, dst, rhs, ux, uy, uz, weight, low, lo, hi):
    for t in range(lo, hi):
        centre, pull = coupling2(src, ux, uy, uz, t, low)
        dst[t] = (1.0 - OMEGA) * centre + weight[t] * (rhs[t] + pull)


def dot(a, b):
    b = b.astype(BF16)
    high = a.astype(BF16)
    rest = a - high.astype(F32)
    middle = rest.astype(BF16)
    low = (rest - middle.astype(F32)).astype(BF16)
    products = [jnp.dot(part, b, preferred_element_type=F32) for part in (low, middle, high)]
    return products[0] + products[1] + products[2]


def pair_matrix(rows, cols, odd):
    k = lax.broadcasted_iota(jnp.int32, (rows, cols), 0)
    j = lax.broadcasted_iota(jnp.int32, (rows, cols), 1)
    hit = (k == 2 * j + 1) if odd else (k // 2 == j)
    return jnp.where(hit, 1.0, 0.0).astype(F32)


def spread_matrix(rows, cols):
    k = lax.broadcasted_iota(jnp.int32, (rows, cols), 0)
    j = lax.broadcasted_iota(jnp.int32, (rows, cols), 1)
    return jnp.where(k == j // 2, 1.0, 0.0).astype(F32)


def conjugate(rhs, coef_ref, out_ref):
    lane = lax.broadcasted_iota(jnp.int32, (NW, 8, 128), 2)
    low, high = lane < 96, lane >= 32
    sink, ux, uy, uz = (coef_ref[:, k] for k in range(4))

    def y_up(v):
        q = pltpu.roll(v, 96, 2)
        return jnp.where(low, q, pltpu.roll(q, 7, 1))

    def y_down(v):
        q = pltpu.roll(v, 32, 2)
        return jnp.where(high, q, pltpu.roll(q, 1, 1))

    def z_up(v):
        return pltpu.roll(v, 127, 2)

    def z_down(v):
        return pltpu.roll(v, 1, 2)

    def total(v):
        parts = [v[k] for k in range(NW)]
        while len(parts) > 1:
            parts = [x + y for x, y in zip(parts[::2], parts[1::2])]
        return jnp.sum(parts[0], axis=(0, 1), keepdims=True)[None]

    edge = jnp.zeros((1, 8, 128), F32)
    dx = jnp.concatenate([edge, ux[:-1]], axis=0)
    diag = sink + (ux + dx) + (uy + y_down(uy)) + (uz + z_down(uz))

    def apply(p):
        above = jnp.concatenate([p[1:], edge], axis=0)
        px = ux * p
        below = jnp.concatenate([edge, px[:-1]], axis=0)
        return diag * p - (
            (ux * above + below)
            + (uy * y_up(p) + y_down(uy * p))
            + (uz * z_up(p) + z_down(uz * p))
        )

    def body(_, carry):
        solved, residual, direction, norm_now = carry
        applied = apply(direction)
        step = norm_now / total(direction * applied)
        solved = solved + step * direction
        residual = residual - step * applied
        norm_next = total(residual * residual)
        direction = residual + (norm_next / norm_now) * direction
        return solved, residual, direction, norm_next

    start = (jnp.zeros_like(rhs), rhs, rhs, total(rhs * rhs))
    solved, residual, direction, norm_now = lax.fori_loop(0, COARSE_ITERS - 1, body, start)
    step = norm_now / total(direction * apply(direction))
    out_ref[...] = solved + step * direction


def kernel(
    dens_in, temp_in, aim_in, sink_in, adj_out, sens_out,
    dens, temp, aim, sink, ux0, uy0, uz0, d0, w0, ua, ub, v0, zs, lift0,
    stage, pairs,
    c1, f1, v1, d1, w1, p1, q1, lift1,
    c2, f2, v2, d2, w2, p2, q2, lift2,
    ga, gb, ra, rb, solved3, rows3, blank,
    in_sem, send_sem, recv_sem,
):
    wide, narrow = lax.axis_index("wide"), lax.axis_index("narrow")
    wire = Wire(wide, narrow, blank, send_sem, recv_sem)
    barrier = pltpu.get_barrier_semaphore()
    peers = greeted()
    for dw, dn in peers:
        pl.semaphore_signal(barrier, inc=1, device_id=wire.peer(dw, dn), device_id_type=MESH)

    own = (pl.ds(4, 8), pl.ds(8, 32))
    loads = []
    for k, (src, dst) in enumerate(
        ((dens_in, dens.at[own]), (sink_in, sink.at[own]), (aim_in, aim.at[own]),
         (temp_in, temp.at[pl.ds(1, 8), pl.ds(8, 32)]))
    ):
        load = pltpu.make_async_copy(src, dst, in_sem.at[k])
        load.start()
        loads.append(load)
    for load in loads:
        load.wait()
    pl.semaphore_wait(barrier, len(peers))

    def halo(ref, own_x, halo_x, width_x, own_y, lead=(), corner=0, group=None, targets=None):
        group = group or wire.group()
        for dw, dn in targets or near_peers(1):
            sx, tx = cut(own_x, halo_x, corner if corner and dn else width_x, dw)
            sy, ty = cut(own_y, 8, 8, dn)
            wire.send(group, ref.at[lead + (sx, sy)], ref.at[lead + (tx, ty)], dw, dn)
        return group

    sides = [(0, 1), (0, -1)]
    ends = [p for p in near_peers(1) if p[0]]
    beside = wire.group()
    for ref in (dens, sink, aim):
        halo(ref, 8, 4, 4, 32, group=beside, targets=sides)
    first = halo(dens, 8, 4, 4, 32, corner=3, targets=ends)
    second = halo(sink, 8, 4, 3, 32, corner=2, targets=ends)
    third = halo(aim, 8, 4, 3, 32, corner=2, targets=ends)
    temps = wire.group()
    for dw, dn in ((1, 0), (-1, 0), (0, 1), (0, -1)):
        sx, tx = cut(8, 1, 1, dw)
        sy, ty = cut(32, 8, 8, dn)
        wire.send(temps, temp.at[sx, sy], temp.at[tx, ty], dw, dn)

    goal_part = jnp.sum(aim[own] * temp[pl.ds(1, 8), pl.ds(8, 32)], axis=0)
    goal_part = jnp.sum(goal_part[:, :128] + goal_part[:, 128:], axis=0, keepdims=True)

    row0 = narrow * 32 - 8 + lax.broadcasted_iota(jnp.int32, (48, 256), 0)
    lane0 = lax.broadcasted_iota(jnp.int32, (48, 256), 1)
    hy = jnp.where((row0 == -1) | (row0 == 255), 0.0, 0.5).astype(F32)
    hz = jnp.where(lane0 == 255, 0.0, 0.5).astype(F32)

    def hx(i):
        g = wide * 8 - 4 + i
        return jnp.where((g == -1) | (g == 127), 0.0, 0.5).astype(F32)

    def conduct(i):
        s = dens[i]
        return FLOOR_CONDUCTION + (1.0 - FLOOR_CONDUCTION) * s * s * s

    s1, s1_odd = pair_matrix(256, 128, False), pair_matrix(256, 128, True)
    def faces(i):
        c = conduct(i)
        ux0[i] = (c + conduct(i + 1)) * hx(i)
        uy0[i] = (c + up_y(c)) * hy
        uz0[i] = (c + up_z(c)) * hz

    def first0(i):
        ua[i] = w0[i] * aim[i]

    level0 = (ux0, uy0, uz0)

    beside.wait_recv()
    layers(4, 11, faces, 4)
    weights(sink, *level0, d0, w0, 5, 11)
    layers(5, 11, first0, 3)
    sweep(ua, ub, aim, *level0, w0, 6, 10)
    sweep(ub, ua, aim, *level0, w0, 7, 9)

    first.wait_recv()
    ux0[0] = (conduct(0) + conduct(1)) * hx(0)
    layers(1, 4, faces, 3)
    layers(11, 15, faces, 4)

    rows = pl.ds(8, 32)
    for k in range(4):
        a, b = 4 + 2 * k, 5 + 2 * k
        stage[pl.ds(32 * k, 32)] = sink[a, rows] + sink[b, rows]
        stage[pl.ds(128 + 32 * k, 32)] = ux0[b, rows]
        stage[pl.ds(256 + 32 * k, 32)] = uy0[a, rows] + uy0[b, rows]
        stage[pl.ds(384 + 32 * k, 32)] = uz0[a, rows] + uz0[b, rows]
    pairs[pl.ds(0, 384)] = dot(stage[pl.ds(0, 384)], s1)
    pairs[pl.ds(384, 128)] = dot(stage[pl.ds(384, 128)], s1_odd)

    def even_odd(base, size):
        return (
            pairs[pl.ds(base, size // 2, stride=2)],
            pairs[pl.ds(base + 1, size // 2, stride=2)],
        )

    own1 = (pl.ds(6, 4), pl.ds(8, 16))
    for k in range(4):
        even, odd = even_odd(128 * k, 128)
        value = (even + odd, 0.5 * (even + odd), 0.5 * odd, 0.5 * (even + odd))[k]
        c1[(k,) + own1] = value.reshape(4, 16, 128)
    coarse1 = halo(c1, 4, 6, 4, 16, (slice(None),))
    for dn in (0, 1, -1):
        sy, ty = cut(16, 8, 8, dn)
        wire.send(coarse1, c1.at[1, pl.ds(9, 1), sy], c1.at[1, pl.ds(1, 1), ty], 2, dn)

    rows1, rows2 = pl.ds(8, 16), pl.ds(8, 8)
    for k in range(2):
        a, b = 6 + 2 * k, 7 + 2 * k
        half = pl.ds(128 * k, 128)
        stage[pl.ds(0, 16), half] = c1[0, a, rows1] + c1[0, b, rows1]
        stage[pl.ds(16, 16), half] = c1[1, b, rows1]
        stage[pl.ds(32, 16), half] = c1[2, a, rows1] + c1[2, b, rows1]
        stage[pl.ds(48, 16), half] = c1[3, a, rows1] + c1[3, b, rows1]
    pairs[pl.ds(0, 48)] = dot(stage[pl.ds(0, 48)], s1)
    pairs[pl.ds(48, 16)] = dot(stage[pl.ds(48, 16)], s1_odd)
    for k in range(4):
        even, odd = even_odd(16 * k, 16)
        value = (even + odd, 0.5 * (even + odd), 0.5 * odd, 0.5 * (even + odd))[k]
        c2[k, 3, rows2] = value

    def blocks2(ref, lead=()):
        group = wire.group()
        for dw, dn in near_peers(3):
            dst = ref.at[lead + (3 - dw, pl.ds(8 - 8 * dn, 8))]
            wire.send(group, ref.at[lead + (3, rows2)], dst, dw, dn)
        return group

    k3 = lax.broadcasted_iota(jnp.int32, (128, 128), 0)
    j3 = lax.broadcasted_iota(jnp.int32, (128, 128), 1)
    pair3 = (k3 % 64) // 2 == j3 % 32
    s3 = jnp.where(pair3, 1.0, 0.0).astype(F32)
    s3_upper = jnp.where(pair3 & (k3 >= 64), 1.0, 0.0).astype(F32)
    s3_odd = jnp.where(k3 % 64 == 2 * (j3 % 32) + 1, 1.0, 0.0).astype(F32)
    sub8 = lax.broadcasted_iota(jnp.int32, (8, 128), 0)
    lane8 = lax.broadcasted_iota(jnp.int32, (8, 128), 1)
    both_y = sub8 // 2 == lane8 // 32
    odd_y = sub8 == 2 * (lane8 // 32) + 1
    mine = sub8 == narrow

    def as_tile(row):
        return jnp.where(mine, jnp.broadcast_to(row, (8, 128)), 0.0)

    def to_row(values, matrix, mask):
        return jnp.sum(jnp.where(mask, dot(values, matrix), 0.0), axis=0, keepdims=True)

    tiles3 = (
        to_row(c2[0, 3, rows2], s3, both_y),
        0.5 * to_row(c2[1, 3, rows2], s3_upper, both_y),
        0.5 * to_row(c2[2, 3, rows2], s3, odd_y),
        0.5 * to_row(c2[3, 3, rows2], s3_odd, both_y),
        goal_part,
    )
    for k in range(5):
        ga[narrow, k] = as_tile(tiles3[k])
    def along_narrow(ref):
        group = wire.group()
        for dn in range(1, NN):
            wire.send(group, ref.at[narrow], ref.at[narrow], 0, dn)
        return group

    def along_wide(ref):
        group = wire.group()
        for dw in range(1, NW):
            wire.send(group, ref.at[wide], ref.at[wide], dw, 0)
        return group

    gather_a = along_narrow(ga)

    second.wait_recv()
    weights(sink, *level0, d0, w0, 1, 5)
    weights(sink, *level0, d0, w0, 11, 15)
    third.wait_recv()
    layers(1, 5, first0, 4)
    layers(11, 15, first0, 4)
    sweep(ua, ub, aim, *level0, w0, 2, 6)
    sweep(ua, ub, aim, *level0, w0, 10, 14)
    sweep(ub, ua, aim, *level0, w0, 3, 7)
    sweep(ub, ua, aim, *level0, w0, 9, 13)

    def restrict0(k, carry):
        a = 4 + 2 * k
        r = residual_at(ua, aim, ux0, uy0, uz0, d0, a) + residual_at(
            ua, aim, ux0, uy0, uz0, d0, a + 1
        )
        stage[pl.ds(pl.multiple_of(32 * k, 32), 32)] = r[8:40]
        return carry

    lax.fori_loop(0, 4, restrict0, 0)
    pairs[pl.ds(0, 128)] = dot(stage[pl.ds(0, 128)], s1)
    even, odd = even_odd(0, 128)
    f1[own1] = (even + odd).reshape(4, 16, 128)
    right1 = halo(f1, 4, 6, 4, 16)
    v0[own] = ua[own]
    coarse2 = blocks2(c2, (slice(None),))
    gather_a.wait_recv()
    gb[wide] = jnp.sum(ga[...], axis=0)


    coarse1.wait_recv()
    weights(c1.at[0], c1.at[1], c1.at[2], c1.at[3], d1, w1, 2, 14)

    right1.wait_recv()

    level1 = (c1.at[1], c1.at[2], c1.at[3])

    def first1(i):
        p1[i] = w1[i] * f1[i]

    layers(3, 13, first1, 5)
    sweep(p1, q1, f1, *level1, w1, 4, 12)
    sweep(q1, p1, f1, *level1, w1, 5, 11)

    for k in range(2):
        a = 6 + 2 * k
        r = residual_at(p1, f1, *level1, d1, a) + residual_at(p1, f1, *level1, d1, a + 1)
        stage[pl.ds(0, 16), pl.ds(128 * k, 128)] = r[8:24]
    pairs[pl.ds(0, 16)] = dot(stage[pl.ds(0, 16)], s1)
    even, odd = even_odd(0, 16)
    f2[3, rows2] = even + odd
    right2 = blocks2(f2)
    before0 = halo(v0, 8, 4, 4, 32, corner=3)
    gather_b = along_wide(gb)
    coarse2.wait_recv()
    low2 = lax.broadcasted_iota(jnp.int32, (24, 128), 1) < 64
    for t in range(7):
        ux, uy, uz = c2[1, t], c2[2, t], c2[3, t]
        ux = ux + previous_x(ux, c2[1, max(t - 1, 0)], low2)
        d2[t] = c2[0, t] + ux + (uy + down_y(uy)) + (uz + down_z(uz))
        w2[t] = OMEGA / d2[t]

    right2.wait_recv()
    level2 = (c2.at[1], c2.at[2], c2.at[3])

    for t in range(1, 6):
        p2[t] = w2[t] * f2[t]
    sweep2(p2, q2, f2, *level2, w2, low2, 2, 5)
    sweep2(q2, p2, f2, *level2, w2, low2, 2, 5)
    centre, pull = coupling2(p2, *level2, 3, low2)
    r = f2[3] + pull - d2[3] * centre
    old = len(wire.groups)
    ra[narrow] = as_tile(to_row(r[8:16], s3, both_y))
    right3 = along_narrow(ra)
    v2[3, rows2] = p2[3, rows2]
    before2 = blocks2(v2)
    right3.wait_recv()
    rb[wide] = jnp.sum(ra[...], axis=0)
    right3 = along_wide(rb)
    v1[own1] = p1[own1]
    before1 = halo(v1, 4, 6, 4, 16)
    for dw, src, dst in ((2, 9, 1), (-2, 6, 14)):
        for dn in (0, 1, -1):
            sy, ty = cut(16, 8, 8, dn)
            wire.send(before1, v1.at[pl.ds(src, 1), sy], v1.at[pl.ds(dst, 1), ty], dw, dn)
    wire.flush(old)
    gather_b.wait_recv()
    goal = jnp.sum(jnp.sum(gb[:, 4], axis=0), axis=(0, 1), keepdims=True)
    right3.wait_recv()

    conjugate(rb[...], gb, solved3)

    for a in range(7):
        layer = lax.rem(wide + (a - 3 + NW), NW)
        for b in range(3):
            line = lax.rem(narrow + (b - 1 + NN), NN)
            row = jnp.broadcast_to(solved3[layer, pl.ds(line, 1)], (8, 128))
            rows3[pl.ds(24 * a + 8 * b, 8)] = jnp.where(both_y, row, 0.0)
    e3 = jnp.where(k3 % 32 == (j3 % 64) // 2, 1.0, 0.0).astype(F32)
    lift2[...] = dot(rows3[...], e3).reshape(7, 24, 128)
    before2.wait_recv()

    for t in range(7):
        p2[t] = v2[t] + lift2[t]
    sweep2(p2, q2, f2, *level2, w2, low2, 0, 7)
    sweep2(q2, p2, f2, *level2, w2, low2, 1, 6)
    sweep2(p2, q2, f2, *level2, w2, low2, 1, 6)

    e1 = spread_matrix(128, 256)
    lift = dot(q2[pl.ds(1, 5)].reshape(120, 128), e1).reshape(5, 24, 256)
    for t in range(5):
        for half in range(2):
            part = lift[t, 4:20, 128 * half : 128 * half + 128]
            lift1[2 * t + half, pl.ds(0, 16, stride=2)] = part
            lift1[2 * t + half, pl.ds(1, 16, stride=2)] = part
    before1.wait_recv()

    for i in range(1, 15):
        p1[i] = v1[i] + lift1[1 + i // 2]
    sweep(p1, q1, f1, *level1, w1, 2, 14)
    sweep(q1, p1, f1, *level1, w1, 3, 13)
    sweep(p1, q1, f1, *level1, w1, 4, 12)

    lift = dot(q1[pl.ds(4, 8), pl.ds(0, 32)].reshape(256, 128), e1).reshape(8, 32, 256)
    before0.wait_recv()
    for a in range(8):
        for half in range(2):
            part = lift[a, 4:28, 128 * half : 128 * half + 128]
            lift0[a, half, pl.ds(0, 24, stride=2)] = part
            lift0[a, half, pl.ds(1, 24, stride=2)] = part

    def correct0(k):
        both = jnp.concatenate([lift0[k, 0], lift0[k, 1]], axis=1)
        ua[2 * k] = v0[2 * k] + both
        ua[2 * k + 1] = v0[2 * k + 1] + both

    layers(0, 8, correct0, 4)
    sweep(ua, ub, aim, ux0, uy0, uz0, w0, 1, 15)
    sweep(ub, ua, aim, ux0, uy0, uz0, w0, 2, 14)

    temps.wait_recv()
    scale = (-0.5 * 3.0 * (1.0 - FLOOR_CONDUCTION)) * (CELLS / goal)
    my, mz = 2.0 * hy, 2.0 * hz

    def face_x(i):
        return (temp[i - 3] - temp[i - 2]) * (ub[i] - ub[i + 1]) * (2.0 * hx(i))

    def slope(i, below):
        t, a, s = temp[i - 3], ub[i], dens[i]
        above = face_x(i)
        fy = (t - up_y(t)) * (a - up_y(a)) * my
        fz = (t - up_z(t)) * (a - up_z(a)) * mz
        raw = (above + below) + (fy + down_y(fy)) + (fz + down_z(fz))
        zs[i, pl.ds(8, 32)] = (raw * scale * s * s)[8:40]
        return above

    sweep(ua, ub, aim, *level0, w0, 3, 9)
    below = face_x(3)
    for i in range(4, 8):
        below = slope(i, below)
    scaled = halo(zs, 8, 4, 4, 32, corner=3, targets=[p for p in ends if p[0] < 0])
    sweep(ua, ub, aim, *level0, w0, 9, 13)
    for i in range(8, 12):
        below = slope(i, below)
    halo(zs, 8, 4, 4, 32, corner=3, group=scaled, targets=[p for p in ends if p[0] > 0])
    scaled_beside = halo(zs, 8, 4, 4, 32, targets=sides)
    adj_out[...] = ub[own]

    first_layer = jnp.where(wide == 0, 4, 0)
    last_layer = jnp.where(wide == NW - 1, 11, 15)
    top, bottom = row0 == 255, row0 == 0
    right, left = lane0 == 255, lane0 == 0
    c1_filter = FILTER_OMEGA / (1.0 + 6.0 * STRENGTH)

    def filter_at(src, i):
        z = src[i]
        near = src[jnp.minimum(i + 1, last_layer)] + src[jnp.maximum(i - 1, first_layer)]
        near = near + (jnp.where(top, z, up_y(z)) + jnp.where(bottom, z, down_y(z)))
        near = near + (jnp.where(right, z, up_z(z)) + jnp.where(left, z, down_z(z)))
        return (1.0 - FILTER_OMEGA) * z + c1_filter * (zs[i] + STRENGTH * near)

    def filter_sweep(src, dst, lo, hi):
        def body(i):
            dst[i] = filter_at(src, i)

        layers(lo, hi, body, 4)

    scaled_beside.wait_recv()
    filter_sweep(zs, ua, 5, 11)
    filter_sweep(ua, ub, 6, 10)
    filter_sweep(ub, ua, 7, 9)
    scaled.wait_recv()
    filter_sweep(zs, ua, 1, 5)
    filter_sweep(zs, ua, 11, 15)
    filter_sweep(ua, ub, 2, 6)
    filter_sweep(ua, ub, 10, 14)
    filter_sweep(ub, ua, 3, 7)
    filter_sweep(ub, ua, 9, 13)

    def last_filter(i):
        sens_out[i - 4] = filter_at(ua, i)[8:40]

    layers(4, 12, last_filter, 4)
    wire.flush(len(wire.groups))


def local(density, temperature, aim, sink):
    vmem = lambda *shape: pltpu.VMEM(shape, F32)
    level0 = (16, 48, 256)
    level1 = (16, 32, 128)
    level2 = (7, 24, 128)
    scratch = [vmem(*level0), vmem(10, 48, 256)] + [vmem(*level0)] * 11 + [vmem(8, 2, 48, 128)]
    scratch += [vmem(512, 256), vmem(512, 128)]
    scratch += [vmem(4, *level1)] + [vmem(*level1)] * 6 + [vmem(10, 32, 128)]
    scratch += [vmem(4, *level2)] + [vmem(*level2)] * 6 + [vmem(7, 24, 128)]
    scratch += [vmem(NN, 5, 8, 128), vmem(NW, 5, 8, 128), vmem(NN, 8, 128), vmem(NW, 8, 128)]
    scratch += [vmem(NW, 8, 128), vmem(168, 128), vmem(BLANK_TILES, 8, 128)]
    scratch += [
        pltpu.SemaphoreType.DMA((4,)),
        pltpu.SemaphoreType.DMA((N_GROUPS,)),
        pltpu.SemaphoreType.DMA((N_GROUPS,)),
    ]
    block = jax.ShapeDtypeStruct((8, 32, 256), F32)
    whole = pl.BlockSpec(memory_space=pltpu.VMEM)
    return pl.pallas_call(
        kernel,
        out_shape=(block, block),
        in_specs=[pl.BlockSpec(memory_space=pl.ANY)] * 4,
        out_specs=(whole, whole),
        scratch_shapes=scratch,
        compiler_params=pltpu.CompilerParams(
            collective_id=0, has_side_effects=True, vmem_limit_bytes=62 * 2**20
        ),
    )(density, temperature, aim, sink)


def solution(mesh):
    placed = P("wide", "narrow", None)
    return jax.shard_map(
        local,
        mesh=mesh,
        in_specs=(placed,) * 4,
        out_specs=(placed, placed),
        check_vma=False,
    )
```

profile of v0, /device:TPU:1, one launch (start us, length us, event | category | flops | bytes accessed | tf_op | source)
XLA Modules:
  0.0 66.7 jit_solution(8536188383380464542)
XLA Ops:
  0.6 63.6 %shard_map.59 = (f32[8,32,256]{2,1,0:T(8,128)}, f32[8,32,256]{2,1,0:T(8,128)}) custom-call(f32[8,32,256]{2,1,0:T(8,128)} %dens_in.1, f32[8,32,256]{2,1,0:T(8,128)} %temp_in.1, f32[8,32,256]{2,1,0:T(8,128)} %aim_in.1, f32[8,32,256]{2,1,0:T(8,128)} %sink_in.1), custom_call_target="tpu_custom_call" | custom-call | tf_op jit(solution)/shard_map/pallas_call | solution.py:670
  64.3 0.0 copy-start
  64.3 1.7 %copy.8 = f32[8,32,256]{2,1,0:T(8,128)} copy(f32[8,32,256]{2,1,0:T(8,128)} %get-tuple-element.4) | data formatting | bytes 524288
  66.0 0.0 copy-done
  66.0 0.7 %copy.9 = f32[8,32,256]{2,1,0:T(8,128)} copy(f32[8,32,256]{2,1,0:T(8,128)S(1)} %copy-done) | data formatting | bytes 524288
Async XLA Ops:
  64.3 1.7 %copy-start = (f32[8,32,256]{2,1,0:T(8,128)S(1)}, f32[8,32,256]{2,1,0:T(8,128)}, u32[]{:S(2)}) copy-start(f32[8,32,256]{2,1,0:T(8,128)} %get-tuple-element.5) | copy-start | bytes 786436
where the time goes:
time: 66.8 us; the launch traced here: 66.7 us
  Pallas kernels  63.6 us (95%)
  local copies, waits for them, and re-layouts  2.42 us (4%)
    pallas_call x1, Pallas kernels, local(): pl.pallas_call(kernel, out_shape=(block, block), in_specs=[pl.BlockSpec(m...  63.6 us
    unnamed x4, local copies, waits for them, and re-layouts  2.42 us

commit v1 on v0

--- a/solution.py
+++ b/solution.py
@@ -19,7 +19,7 @@
 CELLS = 128 * 256 * 256
 F32 = jnp.float32
 BF16 = jnp.bfloat16
-N_GROUPS = 18
+N_GROUPS = 19
 BLANK_TILES = 200
 UNROLL = {48: 4, 32: 8}
 
@@ -264,12 +264,12 @@
 
 
 def kernel(
-    dens_in, temp_in, aim_in, sink_in, adj_out, sens_out,
+    dens_in, temp_in, aim_in, sink_in, outs,
     dens, temp, aim, sink, ux0, uy0, uz0, d0, w0, ua, ub, v0, zs, lift0,
     stage, pairs,
     c1, f1, v1, d1, w1, p1, q1, lift1,
     c2, f2, v2, d2, w2, p2, q2, lift2,
-    ga, gb, ra, rb, solved3, rows3, blank,
+    ga, gb, ra, rb, solved3, rows3, blank, corner_out, corner_in,
     in_sem, send_sem, recv_sem,
 ):
     wide, narrow = lax.axis_index("wide"), lax.axis_index("narrow")
@@ -305,9 +305,26 @@
     beside = wire.group()
     for ref in (dens, sink, aim):
         halo(ref, 8, 4, 4, 32, group=beside, targets=sides)
-    first = halo(dens, 8, 4, 4, 32, corner=3, targets=ends)
-    second = halo(sink, 8, 4, 3, 32, corner=2, targets=ends)
-    third = halo(aim, 8, 4, 3, 32, corner=2, targets=ends)
+    straight = [p for p in ends if not p[1]]
+    corners = [p for p in ends if p[1]]
+    first = halo(dens, 8, 4, 4, 32, targets=straight)
+
+    row8 = lax.broadcasted_iota(jnp.int32, (8, 256), 0)
+    packed = wire.group()
+    for q, (dw, dn) in enumerate(corners):
+        edge = pl.ds(32, 8) if dn > 0 else pl.ds(8, 8)
+        for j in range(3):
+            layer = (9 if dw > 0 else 4) + j
+            d, s, a = dens[layer, edge], sink[layer, edge], aim[layer, edge]
+            if dn > 0:
+                rest = jnp.where(row8 >= 3, pltpu.roll(s, 5, 0), pltpu.roll(a, 3, 0))
+                corner_out[q, j] = jnp.where(row8 >= 5, d, rest)
+            else:
+                rest = jnp.where(row8 < 5, pltpu.roll(s, 3, 0), pltpu.roll(a, 5, 0))
+                corner_out[q, j] = jnp.where(row8 < 3, d, rest)
+        wire.send(packed, corner_out.at[q], corner_in.at[q], dw, dn)
+    second = halo(sink, 8, 4, 3, 32, targets=straight)
+    third = halo(aim, 8, 4, 3, 32, targets=straight)
     temps = wire.group()
     for dw, dn in ((1, 0), (-1, 0), (0, 1), (0, -1)):
         sx, tx = cut(8, 1, 1, dw)
@@ -350,6 +367,16 @@
     sweep(ub, ua, aim, *level0, w0, 7, 9)
 
     first.wait_recv()
+    packed.wait_recv()
+    for q, (dw, dn) in enumerate(corners):
+        edge = pl.ds(0, 8) if dn > 0 else pl.ds(40, 8)
+        for j in range(3):
+            layer = (1 if dw > 0 else 12) + j
+            tile = corner_in[q, j]
+            dens[layer, edge] = tile
+            if j != (0 if dw > 0 else 2):
+                sink[layer, edge] = pltpu.roll(tile, 3 if dn > 0 else 5, 0)
+                aim[layer, edge] = pltpu.roll(tile, 5 if dn > 0 else 3, 0)
     ux0[0] = (conduct(0) + conduct(1)) * hx(0)
     layers(1, 4, faces, 3)
     layers(11, 15, faces, 4)
@@ -609,7 +636,9 @@
         below = slope(i, below)
     halo(zs, 8, 4, 4, 32, corner=3, group=scaled, targets=[p for p in ends if p[0] > 0])
     scaled_beside = halo(zs, 8, 4, 4, 32, targets=sides)
-    adj_out[...] = ub[own]
+    v0[own] = ub[own]
+    store_adj = pltpu.make_async_copy(v0.at[own], outs.at[0], in_sem.at[0])
+    store_adj.start()
 
     first_layer = jnp.where(wide == 0, 4, 0)
     last_layer = jnp.where(wide == NW - 1, 11, 15)
@@ -643,10 +672,18 @@
     filter_sweep(ub, ua, 9, 13)
 
     def last_filter(i):
-        sens_out[i - 4] = filter_at(ua, i)[8:40]
-
-    layers(4, 12, last_filter, 4)
+        ub[i] = filter_at(ua, i)
+
+    stores = [store_adj]
+    for k in range(2):
+        layers(4 + 4 * k, 8 + 4 * k, last_filter, 4)
+        part = ub.at[pl.ds(4 + 4 * k, 4), pl.ds(8, 32)]
+        store = pltpu.make_async_copy(part, outs.at[1, pl.ds(4 * k, 4)], in_sem.at[1 + k])
+        store.start()
+        stores.append(store)
     wire.flush(len(wire.groups))
+    for store in stores:
+        store.wait()
 
 
 def local(density, temperature, aim, sink):
@@ -660,23 +697,24 @@
     scratch += [vmem(4, *level2)] + [vmem(*level2)] * 6 + [vmem(7, 24, 128)]
     scratch += [vmem(NN, 5, 8, 128), vmem(NW, 5, 8, 128), vmem(NN, 8, 128), vmem(NW, 8, 128)]
     scratch += [vmem(NW, 8, 128), vmem(168, 128), vmem(BLANK_TILES, 8, 128)]
+    scratch += [vmem(4, 3, 8, 256)] * 2
     scratch += [
         pltpu.SemaphoreType.DMA((4,)),
         pltpu.SemaphoreType.DMA((N_GROUPS,)),
         pltpu.SemaphoreType.DMA((N_GROUPS,)),
     ]
-    block = jax.ShapeDtypeStruct((8, 32, 256), F32)
-    whole = pl.BlockSpec(memory_space=pltpu.VMEM)
-    return pl.pallas_call(
+    block = jax.ShapeDtypeStruct((2, 8, 32, 256), F32)
+    both = pl.pallas_call(
         kernel,
-        out_shape=(block, block),
+        out_shape=block,
         in_specs=[pl.BlockSpec(memory_space=pl.ANY)] * 4,
-        out_specs=(whole, whole),
+        out_specs=pl.BlockSpec(memory_space=pl.ANY),
         scratch_shapes=scratch,
         compiler_params=pltpu.CompilerParams(
             collective_id=0, has_side_effects=True, vmem_limit_bytes=62 * 2**20
         ),
     )(density, temperature, aim, sink)
+    return both[0], both[1]
 
 
 def solution(mesh):

time: 66.8 us -> 64.8 us (0.970)
  Pallas kernels: 63.6 us -> 62.1 us
    unnamed x4 -> x0, local copies, waits for them, and re-layouts: 2.42 us -> none
    squeeze x0 -> x1, local copies, waits for them, and re-layouts: none -> 1.87 us  [local(): return (both[0], both[1])]
    pallas_call x1, Pallas kernels: 63.6 us -> 62.1 us  [local(): pl.pallas_call(kernel, out_shape=block, in_specs=[pl.BlockSpec(memory_spa...]
where the time goes in v1:
time: 64.8 us; the launch traced here: 64.7 us
  Pallas kernels  62.1 us (96%)
  local copies, waits for them, and re-layouts  1.87 us (3%)
    pallas_call x1, Pallas kernels, local(): pl.pallas_call(kernel, out_shape=block, in_specs=[pl.BlockSpec(memory_spa...  62.1 us
    squeeze x1, local copies, waits for them, and re-layouts, local(): return (both[0], both[1])  1.87 us

profile of v1, /device:TPU:1, one launch (start us, length us, event | category | flops | bytes accessed | tf_op | source)
XLA Modules:
  0.0 64.7 jit_solution(13175436031213199229)
XLA Ops:
  0.6 62.1 %shard_map.59 = f32[2,8,32,256]{3,2,1,0:T(8,128)} custom-call(f32[8,32,256]{2,1,0:T(8,128)} %dens_in.1, f32[8,32,256]{2,1,0:T(8,128)} %temp_in.1, f32[8,32,256]{2,1,0:T(8,128)} %aim_in.1, f32[8,32,256]{2,1,0:T(8,128)} %sink_in.1), custom_call_target="tpu_custom_call" | custom-call | tf_op jit(solution)/shard_map/pallas_call | solution.py:707
  62.8 1.9 %slice_bitcast_fusion = (f32[8,32,256]{2,1,0:T(8,128)}, f32[8,32,256]{2,1,0:T(8,128)}) fusion(f32[2,8,32,256]{3,2,1,0:T(8,128)} %shard_map.59), kind=kLoop, calls=%fused_computation | loop fusion | bytes 1048576 | tf_op jit(solution)/shard_map/squeeze | solution.py:717

commit v2 on v1

--- a/solution.py
+++ b/solution.py
@@ -481,15 +481,12 @@
     sweep(ub, ua, aim, *level0, w0, 3, 7)
     sweep(ub, ua, aim, *level0, w0, 9, 13)
 
-    def restrict0(k, carry):
+    for k in range(4):
         a = 4 + 2 * k
         r = residual_at(ua, aim, ux0, uy0, uz0, d0, a) + residual_at(
             ua, aim, ux0, uy0, uz0, d0, a + 1
         )
-        stage[pl.ds(pl.multiple_of(32 * k, 32), 32)] = r[8:40]
-        return carry
-
-    lax.fori_loop(0, 4, restrict0, 0)
+        stage[pl.ds(32 * k, 32)] = r[8:40]
     pairs[pl.ds(0, 128)] = dot(stage[pl.ds(0, 128)], s1)
     even, odd = even_odd(0, 128)
     f1[own1] = (even + odd).reshape(4, 16, 128)

time: 64.8 us -> 64.8 us (level)
  no operation moved by 1% of the time
where the time goes in v2:
time: 64.8 us; the launch traced here: 64.7 us
  Pallas kernels  62.1 us (96%)
  local copies, waits for them, and re-layouts  1.87 us (3%)
    pallas_call x1, Pallas kernels, local(): pl.pallas_call(kernel, out_shape=block, in_specs=[pl.BlockSpec(memory_spa...  62.1 us
    squeeze x1, local copies, waits for them, and re-layouts, local(): return (both[0], both[1])  1.87 us

profile of v2, /device:TPU:1, one launch (start us, length us, event | category | flops | bytes accessed | tf_op | source)
XLA Modules:
  0.0 64.7 jit_solution(506859251836215848)
XLA Ops:
  0.6 62.1 %shard_map.59 = f32[2,8,32,256]{3,2,1,0:T(8,128)} custom-call(f32[8,32,256]{2,1,0:T(8,128)} %dens_in.1, f32[8,32,256]{2,1,0:T(8,128)} %temp_in.1, f32[8,32,256]{2,1,0:T(8,128)} %aim_in.1, f32[8,32,256]{2,1,0:T(8,128)} %sink_in.1), custom_call_target="tpu_custom_call" | custom-call | tf_op jit(solution)/shard_map/pallas_call | solution.py:704
  62.8 1.9 %slice_bitcast_fusion = (f32[8,32,256]{2,1,0:T(8,128)}, f32[8,32,256]{2,1,0:T(8,128)}) fusion(f32[2,8,32,256]{3,2,1,0:T(8,128)} %shard_map.59), kind=kLoop, calls=%fused_computation | loop fusion | bytes 1048576 | tf_op jit(solution)/shard_map/squeeze | solution.py:714
